TPU v7x, 512 devices: a whole 4x4x16 slice. The times are simulated.
512 devices in a mesh: layer: 2 (over core), row: 64 (over z, y), rep: 4 (over x).
Axes of the slice: x: 4, y: 4, z: 16, core: 2. Of those that a mesh axis runs over, the one named last changes fastest.
Arguments:
- features: bfloat16 [32768, 256], P(('row', 'rep')), may hold values from -6 to 6
- class_ids: int32 [32768], P(('row', 'rep')), may hold values from 0 to 256
- label_table: bfloat16 [256, 256], replicated, may hold values from -3 to 3
- self_weight: bfloat16 [2, 256, 256], P('layer'), may hold values from -0.375 to 0.375
- neighbor_weight: bfloat16 [2, 256, 256], P('layer'), may hold values from -0.375 to 0.375
- norm_scale: float32 [256], replicated, may hold values from 0.1 to 1.9
- tile_values: bfloat16 [64, 4, 32, 128, 128], P('row', 'rep')
- tile_block_row: int32 [64, 4, 32], P('row', 'rep'), may hold values from 0 to 3, as said below
- tile_section: int32 [64, 4, 32], P('row', 'rep'), may hold values from 0 to 63
- tile_count: int32 [64, 4], P('row', 'rep'), may hold values from 4 to 32, as said below
Outputs:
- hidden_states: bfloat16 [2, 32768, 256], P('layer', ('row', 'rep'))
Inputs may be any that keep to these rules, and one draw needn't show every extreme that they name: `class_ids`: 256 marks a node without a label. `tile_block_row`: slots 0 to 3 of every device name block rows 0 to 3 in order. `tile_count`: at least 4; 32 on some device.
All inputs are finite; a program needn't handle non-finite values.
Results may differ from a plain program's by a relative error of at most 0.0052.
Values may be sent and summed in bfloat16 or wider, within the bound.
A program may use at most 64 MiB of HBM per device.

v0:
```python
import jax
import jax.numpy as jnp
from jax import lax
from jax.sharding import PartitionSpec as P


def settle(mixture, norm_scale, first):
    if first:
        active = jnp.maximum(mixture, 0.0)
        center = active - jnp.mean(active, axis=-1, keepdims=True)
        spread = jnp.mean(center * center, axis=-1, keepdims=True)
        return (center * lax.rsqrt(spread + 1e-05) * norm_scale).astype(jnp.bfloat16)
    return mixture.astype(jnp.bfloat16)


def body(
    features,
    class_ids,
    label_table,
    self_weight,
    neighbor_weight,
    norm_scale,
    tile_values,
    tile_block_row,
    tile_section,
    tile_count,
):
    which_layer = lax.axis_index("layer")
    groups = lax.axis_size("row")
    splits = lax.axis_size("rep")
    tile_data = tile_values[0, 0]
    block_rows = tile_block_row[0, 0]
    sections = tile_section[0, 0]
    filled = tile_count[0, 0]
    slot_total = tile_data.shape[0]
    tile_edge = tile_data.shape[1]
    hidden_dim = features.shape[1]
    classes = label_table.shape[0]
    one_hot = (class_ids[:, None] == jnp.arange(classes, dtype=jnp.int32)[None, :]).astype(
        jnp.bfloat16
    )
    inputs = (
        features.astype(jnp.float32)
        + jnp.dot(one_hot, label_table, preferred_element_type=jnp.float32)
    ).astype(jnp.bfloat16)
    slot_ids = jnp.arange(slot_total, dtype=jnp.int32)
    targets = jnp.arange(splits, dtype=jnp.int32)

    def placement(keep_mask):
        live = jnp.logical_and(slot_ids < filled, keep_mask)
        return jnp.logical_and(block_rows[None, :] == targets[:, None], live[None, :]).astype(
            jnp.float32
        )

    outcomes = []
    both_self, both_neigh = (
        lax.all_gather(self_weight, "layer", axis=0, tiled=True),
        lax.all_gather(neighbor_weight, "layer", axis=0, tiled=True),
    )
    keep_mask = slot_ids % 2 == which_layer
    half_rows = tile_edge // 2

    def regroup(partial_value):
        shaped = partial_value.reshape((splits, 2, half_rows) + partial_value.shape[1:])
        return jnp.swapaxes(shaped, 0, 1).reshape(partial_value.shape)

    tile_sums = jnp.sum(tile_data, axis=-1, dtype=jnp.float32)
    row_sums = regroup(
        jnp.dot(placement(keep_mask), tile_sums, precision=lax.Precision.HIGHEST).reshape(
            splits * tile_edge
        )
    )
    current = inputs
    for layer_no in range(2):
        gathered = lax.all_gather(current, "row", axis=0, tiled=True)
        panel_rows = gathered.reshape(groups, tile_edge, hidden_dim)
        weights_on = placement(keep_mask)

        def add_tiles(batch_no, running):
            offset = batch_no * 8
            tile_batch = lax.dynamic_slice_in_dim(tile_data, offset, 8, 0)
            where_from = lax.dynamic_slice_in_dim(sections, offset, 8, 0)
            onto_rows = lax.dynamic_slice_in_dim(weights_on, offset, 8, 1)
            sources = panel_rows[where_from]
            products = jnp.einsum(
                "kab,kbf->kaf", tile_batch, sources, preferred_element_type=jnp.float32
            )
            return running + jnp.einsum(
                "sk,kaf->saf", onto_rows, products, precision=lax.Precision.HIGHEST
            )

        running = jnp.zeros((splits, tile_edge, hidden_dim), jnp.float32)
        running = lax.fori_loop(0, slot_total // 8, add_tiles, running)
        partial_value = regroup(running.reshape(splits * tile_edge, hidden_dim))
        if layer_no == 0:
            summed, degree = (
                lax.psum_scatter(partial_value, ("layer", "rep"), scatter_dimension=0, tiled=True),
                lax.psum_scatter(row_sums, ("layer", "rep"), scatter_dimension=0, tiled=True),
            )
        else:
            summed = lax.psum_scatter(
                partial_value, ("layer", "rep"), scatter_dimension=0, tiled=True
            )
        own_rows = lax.dynamic_slice_in_dim(current, which_layer * half_rows, half_rows, 0)
        neighbor = (summed * lax.rsqrt(degree)[:, None]).astype(jnp.bfloat16)
        mixture = jnp.dot(
            own_rows, both_self[layer_no], preferred_element_type=jnp.float32
        ) + jnp.dot(neighbor, both_neigh[layer_no], preferred_element_type=jnp.float32)
        current = lax.all_gather(
            settle(mixture, norm_scale, layer_no == 0), "layer", axis=0, tiled=True
        )
        outcomes.append(current)
    selected = jnp.where(which_layer == 0, outcomes[0], outcomes[1])
    return selected[None]


def solution(mesh):
    return jax.shard_map(
        body,
        mesh=mesh,
        in_specs=(
            P(("row", "rep"), None),
            P(("row", "rep")),
            P(),
            P("layer", None, None),
            P("layer", None, None),
            P(),
            P("row", "rep", None, None, None),
            P("row", "rep", None),
            P("row", "rep", None),
            P("row", "rep"),
        ),
        out_specs=P("layer", ("row", "rep"), None),
        check_vma=False,
    )
```

profile of v0, /device:TPU:1, one launch (start us, length us, event | category | flops | bytes accessed | tf_op | source)
XLA Modules:
  0.0 444.6 jit_solution(2282991943792585392)
XLA Ops:
  6.5 0.9 copy-done
  7.4 1.7 fusion.14
  9.9 0.7 fusion.28
  10.6 143.6 %all-gather.3.cloned.1.call-done = bf16[8192,256]{1,0:T(8,128)(2,1)} async-done(((bf16[128,256]{1,0:T(8,128)(2,1)}), bf16[8192,256]{1,0:T(8,128)(2,1)}) %all-gather.3.cloned.1.call-update) | async-done | bytes 4194320 | tf_op jit(solution)/shard_map/all_gather | solution.py:75
  154.1 26.5 %while.28 = (s32[]{:T(128)}, f32[4,128,256]{2,0,1:T(4,128)S(1)}, f32[4,32]{1,0:T(4,128)S(1)}, bf16[32,128,128]{2,1,0:T(8,128)(2,1)}, s32[32]{0:T(128)}, /*index=...) while((s32[]{:T(128)}, f32[4,128,256]{2,0,1:T(4,128)S(1)}, ...), condition=%wide.region_1.2_spmd.clone, body=%wide.region_0.1_spmd.clone.sunk | while | flops 79954976 | bytes 4985641 | solution.py:93
  154.1 0.8 compare_select_fusion.4
  154.9 2.8 gather_fusion
  157.7 1.2 fusion.51
  158.9 1.8 convolution_add_fusion.7
  160.8 0.7 compare_select_fusion.4
  161.5 2.8 gather_fusion
  164.3 1.2 fusion.51
  165.6 1.8 convolution_add_fusion.7
  167.4 0.7 compare_select_fusion.4
  168.2 2.8 gather_fusion
  170.9 1.2 fusion.51
  172.2 1.8 convolution_add_fusion.7
  174.0 0.7 compare_select_fusion.4
  174.8 2.8 gather_fusion
  177.6 1.2 fusion.51
  178.8 1.8 convolution_add_fusion.7
  180.8 0.8 copy.22
  181.7 1.6 convert_reduce_fusion
  183.6 1.3 dynamic-slice
  185.5 23.5 %all-reduce = f32[512]{0:T(512)S(1)} all-reduce(f32[512]{0:T(512)S(1)} %reshape.47), channel_id=3, replica_groups=mesh['layer'=2,'row'=64,'rep'=4] {'layer','rep'}, use_global_device_ids=true, to_apply=%region_4.5.clone | all-reduce | flops 512 | bytes 4096
  209.1 2.0 all_gather.18
  211.0 2.0 all_gather.20
  213.3 11.7 %reduce-scatter.3.cloned.1.call-done = f32[64,256]{1,0:T(8,128)} async-done(((f32[512,256]{1,0:T(8,128)}), f32[64,256]{1,0:T(8,128)}) %reduce-scatter.3.cloned.1.call-update) | async-done | bytes 65552 | tf_op jit(solution)/shard_map/reduce_scatter | solution.py:97
  224.9 1.1 fusion.33
  226.4 2.0 all_gather.21
  228.4 138.1 %all-gather.5.cloned.1.call-done = bf16[8192,256]{1,0:T(8,128)(2,1)} async-done(((bf16[128,256]{1,0:T(8,128)(2,1)}), bf16[8192,256]{1,0:T(8,128)(2,1)}) %all-gather.5.cloned.1.call-update) | async-done | bytes 4194320 | tf_op jit(solution)/shard_map/all_gather | solution.py:75
  366.5 23.9 %while.29 = (s32[]{:T(128)}, f32[4,128,256]{2,0,1:T(4,128)S(1)}, f32[4,32]{1,0:T(4,128)S(1)}, bf16[32,128,128]{2,1,0:T(8,128)(2,1)}, s32[32]{0:T(128)S(1)}, /*in...) while((s32[]{:T(128)}, f32[4,128,256]{2,0,1:T(4,128)S(1)}, ...), condition=%wide.region_8.9_spmd.clone, body=%wide.region_7.8_spmd.clone.sunk | while | flops 79954976 | bytes 4985641 | solution.py:93
  366.6 2.8 gather_fusion.1
  369.4 1.2 fusion.56
  370.6 1.8 convolution_add_fusion.8
  372.6 2.8 gather_fusion.1
  375.3 1.2 fusion.56
  376.6 1.8 convolution_add_fusion.8
  378.5 2.8 gather_fusion.1
  381.3 1.2 fusion.56
  382.6 1.8 convolution_add_fusion.8
  384.5 2.8 gather_fusion.1
  387.3 1.2 fusion.56
  388.5 1.8 convolution_add_fusion.8
  390.5 0.8 copy.25
  391.5 43.1 %reduce-scatter.5.cloned.1.call-done = f32[64,256]{1,0:T(8,128)} async-done(((f32[512,256]{1,0:T(8,128)}), f32[64,256]{1,0:T(8,128)}) %reduce-scatter.5.cloned.1.call-update) | async-done | bytes 65552 | tf_op jit(solution)/shard_map/reduce_scatter | solution.py:101
  434.6 1.0 fusion.16
  435.6 1.9 all_gather.23
  (51 shorter events, 2.4 us)
Async XLA Ops:
  6.5 0.9 copy-start
  6.5 147.6 %all-gather.3.cloned.1.call-start = ((), (), s32[]{:S(2)}) async-start(), calls=%async_computation.2 | async-start | bytes 4259840 | tf_op jit(solution)/shard_map/all_gather | solution.py:75
  9.2 215.8 %reduce-scatter.3.cloned.1.call-start = ((), (), s32[]{:S(2)}) async-start(), calls=%async_computation.3 | async-start | bytes 589824 | tf_op jit(solution)/shard_map/reduce_scatter | solution.py:97
  154.1 29.3 %copy-start.5 = (s32[1,1,32]{2,1,0:T(1,128)S(1)}, s32[1,1,32]{2,1,0:T(1,128)}, u32[]{:S(2)}) copy-start(s32[1,1,32]{2,1,0:T(1,128)} %param.21) | copy-start | bytes 388
  154.1 54.9 %copy-start.3 = (bf16[1,256,256]{2,1,0:T(8,128)(2,1)S(1)}, bf16[1,256,256]{2,1,0:T(8,128)(2,1)}, u32[]{:S(2)}) copy-start(bf16[1,256,256]{2,1,0:T(8,128)(2,1)} %param.17) | copy-start | bytes 393220
  180.6 30.4 %copy-start.4 = (bf16[1,256,256]{2,1,0:T(8,128)(2,1)S(1)}, bf16[1,256,256]{2,1,0:T(8,128)(2,1)}, u32[]{:S(2)}) copy-start(bf16[1,256,256]{2,1,0:T(8,128)(2,1)} %param.18) | copy-start | bytes 393220
  180.7 32.4 %copy-start.2 = (bf16[128,256]{1,0:T(8,128)(2,1)S(1)}, bf16[128,256]{1,0:T(8,128)(2,1)}, u32[]{:S(2)}) copy-start(bf16[128,256]{1,0:T(8,128)(2,1)} %fusion.14) | copy-start | bytes 196612
  180.7 45.6 %copy-start.6 = (f32[256]{0:T(256)S(1)}, f32[256]{0:T(256)}, u32[]{:S(2)}) copy-start(f32[256]{0:T(256)} %param.19) | copy-start | bytes 3076
  180.7 185.8 %copy-start.7 = (s32[32]{0:T(128)S(1)}, s32[32]{0:T(128)}, u32[]{:S(2)}) copy-start(s32[32]{0:T(128)} %get-tuple-element.445) | copy-start | bytes 388
  181.7 184.9 %all-gather.5.cloned.1.call-start = ((), (), s32[]{:S(2)}) async-start(), calls=%async_computation.4 | async-start | bytes 4259840 | tf_op jit(solution)/shard_map/all_gather | solution.py:75
  228.4 206.2 %reduce-scatter.5.cloned.1.call-start = ((), (), s32[]{:S(2)}) async-start(), calls=%async_computation.5 | async-start | bytes 589824 | tf_op jit(solution)/shard_map/reduce_scatter | solution.py:101
  366.5 24.8 %copy-start.1 = (bf16[128,256]{1,0:T(8,128)(2,1)S(1)}, bf16[128,256]{1,0:T(8,128)(2,1)}, u32[]{:S(2)}) copy-start(bf16[128,256]{1,0:T(8,128)(2,1)} %all_gather.21) | copy-start | bytes 196612
Sparse Core Ops, SparseCore 0:
  10.3 143.7 all-gather.2
  181.8 43.0 reduce-scatter.2
  228.5 137.9 all-gather.4
  391.4 43.0 reduce-scatter.4
where the time goes:
time: 446 us; the launch traced here: 445 us
  waiting for transfers between devices  336 us (75%)
  blocking collectives  31.3 us (7%)
  matrix products  28.9 us (6%)
  local copies, waits for them, and re-layouts  26.5 us (6%)
  between operations  14.6 us (3%)
  other arithmetic  6.51 us (1%)
    all_gather x2, waiting for transfers between devices, body(): gathered = lax.all_gather(current, 'row', axis=0, tiled=True)  282 us
    reduce_scatter x2, waiting for transfers between devices, body(): lax.psum_scatter(partial_value, ('layer', 'rep'), scatter_dimension=0, ti...  54.8 us
    unnamed x1, blocking collectives  23.5 us
    gather x8, local copies, waits for them, and re-layouts, add_tiles(): sources = panel_rows[where_from]  22.1 us
    dot_general x8, matrix products, add_tiles(): jnp.einsum('sk,kaf->saf', onto_rows, products, precision=lax.Precision.HI...  14.7 us
    dot_general x8, matrix products, add_tiles(): jnp.einsum('kab,kbf->kaf', tile_batch, sources, preferred_element_type=jn...  9.92 us
  transfers between devices with their start and end apart: 4, of which 4 were waited for; matrix products, arithmetic and copies ran while one was open for 1% of the time, Pallas kernels for 0%

commit v1 on v0

v1 whole, which is shorter than its diff:
```python
import functools

import jax
import jax.numpy as jnp
from jax import lax
from jax.experimental import pallas as pl
from jax.experimental.pallas import tpu as pltpu
from jax.sharding import PartitionSpec as P

MESH = pl.DeviceIdType.MESH
RING_Y = 4
ROWS_A = 48
F32 = jnp.float32
BF16 = jnp.bfloat16


def kernel(
    ring_z,
    reps,
    features,
    class_ids,
    label_table,
    self_weight,
    neighbor_weight,
    norm_scale,
    tile_values,
    block_row,
    section,
    count,
    out,
    tiles,
    placed,
    panels,
    first_a,
    first_b,
    second_a,
    second_b,
    weights,
    nodes,
    own_product,
    to_send,
    arrived,
    degree,
    degree_arrived,
    send_sem,
    recv_sem,
    tile_sem,
):
    slots = tiles.shape[0]
    edge = tiles.shape[1]
    parts_a, parts_b = (first_a, second_a), (first_b, second_b)
    rows_a, half_f = first_a.shape[1:]
    rows_b = first_b.shape[2]
    half_z = ring_z // 2
    core = lax.axis_index("layer")
    row = lax.axis_index("row")
    rep = lax.axis_index("rep")
    z, y = row // RING_Y, row % RING_Y

    def device(dz=0, dy=0, dr=0, dc=0):
        to_row = ((z + dz + ring_z) % ring_z) * RING_Y + (y + dy + RING_Y) % RING_Y
        return ((core + dc) % 2, to_row, (rep + dr) % reps)

    def z_slot(d):
        d = d % ring_z
        if d < half_z:
            return 2 * d
        return ring_z - 1 if d == half_z else 2 * (ring_z - d) - 1

    started = []

    def send(src, dst, device_id):
        at = len(started)
        copy = pltpu.make_async_remote_copy(
            src_ref=src,
            dst_ref=dst,
            send_sem=send_sem.at[at],
            recv_sem=recv_sem.at[at],
            device_id=device_id,
            device_id_type=MESH,
        )
        copy.start()
        started.append(copy)
        return copy

    tile_copy = pltpu.make_async_copy(tile_values.at[0, 0], tiles, tile_sem)
    tile_copy.start()

    barrier = pltpu.get_barrier_semaphore()
    friends = [device(dz=1), device(dz=-1), device(dy=1), device(dy=-1), device(dy=2), device(dc=1)]
    for j in range(1, reps):
        friends += [device(dr=j), device(dr=j, dc=1)]
    for friend in friends:
        pl.semaphore_signal(barrier, inc=1, device_id=friend, device_id_type=MESH)

    classes = label_table.shape[0]
    one_hot = (
        lax.broadcasted_iota(jnp.int32, (classes, edge), 0) == class_ids[...]
    ).astype(F32).astype(BF16)
    labels = lax.dot_general(
        one_hot, label_table[...], (((0,), (0,)), ((), ())), preferred_element_type=F32
    )
    inputs = (features[...].astype(F32) + labels).astype(BF16)
    nodes[0] = inputs

    def own_half(whole):
        return jnp.where(core == 0, whole[:, :half_f].astype(F32), whole[:, half_f:].astype(F32)).astype(BF16)

    def gather(layer, whole, work):
        a, b = parts_a[layer], parts_b[layer]
        mine = own_half(whole)
        a[0] = mine[:rows_a]
        b[0, 0] = mine[rows_a:]
        if layer == 0:
            pl.semaphore_wait(barrier, len(friends))

        def b_ring(s):
            cut = 48 if rows_b >= 64 else rows_b // 2
            if s < half_z:
                up, down = slice(None), slice(None)
            else:
                up, down = slice(0, cut), slice(cut, rows_b)
            return (
                send(b.at[0, z_slot(1 - s), up], b.at[0, z_slot(-s), up], device(dz=1)),
                send(b.at[0, z_slot(s - 1), down], b.at[0, z_slot(s), down], device(dz=-1)),
            )

        def a_ring(s):
            def block(d, part):
                at = z_slot(d) * RING_Y
                if s < half_z:
                    return a.at[pl.ds(at, RING_Y)]
                return a.at[pl.ds(at + part * (RING_Y // 2), RING_Y // 2)]

            return (
                send(block(1 - s, 0), block(-s, 0), device(dz=1)),
                send(block(s - 1, 1), block(s, 1), device(dz=-1)),
            )

        def b_side(s):
            if s == 0:
                at = pl.ds(0, 1)
            elif s < half_z:
                at = pl.ds(2 * s - 1, 2)
            else:
                at = pl.ds(ring_z - 1, 1)
            copies = [
                send(b.at[0, at], b.at[RING_Y - 1, at], device(dy=1)),
                send(b.at[0, at], b.at[1, at], device(dy=-1)),
            ]
            if s == half_z:
                copies.append(send(b.at[0, at], b.at[2, at], device(dy=2)))
            return copies

        def b_far(s):
            copies = [send(b.at[RING_Y - 1, max(2 * s - 1, 0)], b.at[2, max(2 * s - 1, 0)], device(dy=1))]
            if s > 0:
                copies.append(send(b.at[1, 2 * s], b.at[2, 2 * s], device(dy=-1)))
            return copies

        a_side = [
            send(a.at[0], a.at[(RING_Y - dy) % RING_Y], device(dy=dy)) for dy in (1, -1, 2)
        ]
        b_now = b_ring(1)
        side = b_side(0)
        last = []
        for copy in a_side:
            copy.wait_recv()
        a_now = a_ring(1)
        work(0)
        for s in range(1, half_z + 1):
            for copy in b_now:
                copy.wait_recv()
            if s < half_z:
                b_now = b_ring(s + 1)
            side_next = b_side(s)
            for copy in a_now:
                copy.wait_recv()
            if s < half_z:
                a_now = a_ring(s + 1)
            for copy in side:
                copy.wait_recv()
            last += b_far(s - 1)
            side = side_next
            work(s)
        for copy in side + last:
            copy.wait_recv()

    filled = count[0, 0]
    targets = [(block_row[0, 0, k] - rep + reps) % reps for k in range(slots)]
    per_step = max(slots // 4, 1)
    ones = jnp.ones((per_step * edge, half_f), BF16)
    hidden = []

    def place(step):
        for k in range(step * per_step, (step + 1) * per_step):
            tile = tiles[k]
            for j in range(reps):
                keep = jnp.logical_and(targets[k] == j, k < filled)
                placed[pl.ds(j * edge, edge), pl.ds(k * edge, edge)] = jnp.where(
                    keep, tile, jnp.zeros_like(tile)
                )
        sums = jnp.dot(
            placed[:, pl.ds(step * per_step * edge, per_step * edge)], ones, preferred_element_type=F32
        )
        if step == 0:
            degree[...] = sums
        else:
            degree[...] += sums

    steps = slots // per_step

    def first_work(s):
        if s == 0:
            weights[core, 0] = self_weight[0]
            weights[core, 1] = neighbor_weight[0]
            hidden.append(send(weights.at[core], weights.at[core], device(dc=1)))
            tile_copy.wait()
        if half_z >= 8:
            if 1 <= s <= steps:
                place(s - 1)
            final = s == steps + 1
        else:
            if s == 0:
                for step in range(steps):
                    place(step)
            final = s == 1
        if final:
            for j in range(1, reps):
                hidden.append(
                    send(degree.at[pl.ds(j * edge, edge)], degree_arrived.at[j - 1], device(dr=j))
                )
        if s == half_z:
            hidden[0].wait_recv()
            own_product[...] = jnp.dot(nodes[0], weights[0, 0], preferred_element_type=F32)

    def second_work(s):
        if s == 1:
            own_product[...] = jnp.dot(nodes[1], weights[1, 0], preferred_element_type=F32)

    def aggregate(layer):
        a, b = parts_a[layer], parts_b[layer]
        for k in range(slots):
            d = (section[0, 0, k] // RING_Y - z + ring_z) % ring_z
            e = (section[0, 0, k] % RING_Y - y + RING_Y) % RING_Y
            at = jnp.where(
                d < half_z, 2 * d, jnp.where(d == half_z, ring_z - 1, 2 * (ring_z - d) - 1)
            )
            panels[pl.ds(k * edge, rows_a), :] = a[at * RING_Y + e]
            panels[pl.ds(k * edge + rows_a, rows_b), :] = b[e, at]
        copies = []
        for j in [reps // 2] + [j for j in range(1, reps) if j != reps // 2] + [0]:
            total = jnp.dot(
                placed[pl.ds(j * edge, edge), :], panels[...], preferred_element_type=F32
            ).astype(BF16)
            if j == 0:
                arrived[layer, 0, core] = total
            else:
                to_send[layer, j - 1] = total
            if layer == 0:
                if j > 0:
                    source = to_send.at[layer, j - 1]
                    copies.append(send(source, arrived.at[layer, j, core], device(dr=j)))
                else:
                    source = arrived.at[layer, 0, core]
                copies.append(
                    send(source, arrived.at[layer, j, core], device(dr=j, dc=1))
                )
            elif j > 0:
                copies.append(to_second(j))
                copies[-1].start()
        return copies

    def to_second(j, from_core=None):
        from_core = core if from_core is None else from_core
        at = len(started_slots) + 2 * (j - 1)
        return pltpu.make_async_remote_copy(
            src_ref=to_send.at[1, j - 1],
            dst_ref=arrived.at[1, j, from_core],
            send_sem=send_sem.at[at],
            recv_sem=recv_sem.at[at + from_core],
            device_id=(1,) + device(dr=j)[1:],
            device_id_type=MESH,
        )

    def mixture(layer, scale):
        z_sum = own_product[...]
        for c in range(2):
            near = sum(arrived[layer, j, c].astype(F32) for j in range(reps))
            agg = (near * scale).astype(BF16)
            z_sum = z_sum + jnp.dot(
                agg, weights[layer, 1, c * half_f : (c + 1) * half_f, :], preferred_element_type=F32
            )
        return z_sum

    gather(0, inputs, first_work)
    copies = aggregate(0)
    for copy in hidden[1:] + copies:
        copy.wait_recv()
    total_degree = degree[:edge, :]
    for j in range(1, reps):
        total_degree = total_degree + degree_arrived[j - 1]
    degree[:edge, :] = lax.rsqrt(total_degree)
    active = jnp.maximum(mixture(0, degree[:edge, :]), 0.0)
    center = active - jnp.mean(active, axis=-1, keepdims=True)
    spread = jnp.mean(center * center, axis=-1, keepdims=True)
    first = (center * lax.rsqrt(spread + 1e-05) * norm_scale[...]).astype(BF16)
    nodes[1] = first

    gather(1, first, second_work)
    started_slots = list(started)
    copies = aggregate(1)
    last_at = len(started_slots) + 2 * (reps - 1)
    across = pltpu.make_async_remote_copy(
        src_ref=arrived.at[1, 0, 0],
        dst_ref=arrived.at[1, 0, 0],
        send_sem=send_sem.at[last_at],
        recv_sem=recv_sem.at[last_at],
        device_id=(1, row, rep),
        device_id_type=MESH,
    )

    @pl.when(core == 0)
    def _():
        across.start()
        out[0] = nodes[1]
        across.wait_send()

    @pl.when(core == 1)
    def _():
        for j in range(1, reps):
            for c in range(2):
                to_second(j, c).wait_recv()
        across.wait_recv()
        out[0] = mixture(1, degree[:edge, :]).astype(BF16)

    for copy in started_slots + copies:
        copy.wait_send()


def solution(mesh):
    reps = mesh.shape["rep"]
    ring_z = mesh.shape["row"] // RING_Y

    def body(
        features,
        class_ids,
        label_table,
        self_weight,
        neighbor_weight,
        norm_scale,
        tile_values,
        block_row,
        section,
        count,
    ):
        slots, edge = tile_values.shape[2:4]
        width = features.shape[1]
        half = width // 2
        rows_b = edge - ROWS_A
        vmem = pl.BlockSpec(memory_space=pltpu.VMEM)
        smem = pl.BlockSpec(memory_space=pltpu.SMEM)
        copies = 2 * (3 + 6 * ring_z) + 8 * reps + 16
        return pl.pallas_call(
            functools.partial(kernel, ring_z, reps),
            out_shape=jax.ShapeDtypeStruct((1, edge, width), BF16),
            in_specs=[vmem] * 6 + [pl.BlockSpec(memory_space=pl.ANY)] + [smem] * 3,
            out_specs=vmem,
            scratch_shapes=[
                pltpu.VMEM((slots, edge, edge), BF16),
                pltpu.VMEM((reps * edge, slots * edge), BF16),
                pltpu.VMEM((slots * edge, half), BF16),
                pltpu.VMEM((ring_z * RING_Y, ROWS_A, half), BF16),
                pltpu.VMEM((RING_Y, ring_z, rows_b, half), BF16),
                pltpu.VMEM((ring_z * RING_Y, ROWS_A, half), BF16),
                pltpu.VMEM((RING_Y, ring_z, rows_b, half), BF16),
                pltpu.VMEM((2, 2, width, width), BF16),
                pltpu.VMEM((2, edge, width), BF16),
                pltpu.VMEM((edge, width), F32),
                pltpu.VMEM((2, reps - 1, edge, half), BF16),
                pltpu.VMEM((2, reps, 2, edge, half), BF16),
                pltpu.VMEM((reps * edge, half), F32),
                pltpu.VMEM((reps - 1, edge, half), F32),
                pltpu.SemaphoreType.DMA((copies,)),
                pltpu.SemaphoreType.DMA((copies,)),
                pltpu.SemaphoreType.DMA,
            ],
            compiler_params=pltpu.CompilerParams(
                collective_id=0, has_side_effects=True, vmem_limit_bytes=40 * 2**20
            ),
        )(
            features,
            class_ids.reshape(1, edge),
            label_table,
            self_weight,
            neighbor_weight,
            norm_scale.reshape(1, width),
            tile_values,
            block_row,
            section,
            count,
        )

    return jax.shard_map(
        body,
        mesh=mesh,
        in_specs=(
            P(("row", "rep"), None),
            P(("row", "rep")),
            P(),
            P("layer", None, None),
            P("layer", None, None),
            P(),
            P("row", "rep", None, None, None),
            P("row", "rep", None),
            P("row", "rep", None),
            P("row", "rep"),
        ),
        out_specs=P("layer", ("row", "rep"), None),
        check_vma=False,
    )
```

time: 446 us -> 111 us (0.25)
  waiting for transfers between devices: 336 us -> 0 us
  Pallas kernels: 0 us -> 104 us
  blocking collectives: 31.3 us -> 0 us
  matrix products: 28.9 us -> 0 us
  local copies, waits for them, and re-layouts: 26.5 us -> 6.09 us
  between operations: 14.6 us -> 0.7 us
  other arithmetic: 6.51 us -> 0 us
    all_gather x2 -> x0, waiting for transfers between devices: 282 us -> none  [body(): gathered = lax.all_gather(current, 'row', axis=0, tiled=True)]
    pallas_call x0 -> x1, Pallas kernels: none -> 104 us  [body(): pl.pallas_call(functools.partial(kernel, ring_z, reps), out_shape=jax.Sha...]
    reduce_scatter x2 -> x0, waiting for transfers between devices: 54.8 us -> none  [body(): lax.psum_scatter(partial_value, ('layer', 'rep'), scatter_dimension=0, ti...]
    dot_general x22 -> x0, matrix products: 28.9 us -> none  [the longest x8 14.7 us: add_tiles(): jnp.einsum('sk,kaf->saf', onto_rows, products, precision=lax.Precision.HI...]
    unnamed x1 -> x0, blocking collectives: 23.5 us -> none
    gather x8 -> x0, local copies, waits for them, and re-layouts: 22.1 us -> none  [add_tiles(): sources = panel_rows[where_from]]
    all_gather x4 -> x0, blocking collectives: 7.8 us -> none  [the longest x2 3.84 us: body(): lax.all_gather(settle(mixture, norm_scale, layer_no == 0), 'layer', axis=...]
  transfers between devices with their start and end apart: 4 -> 0, of which waited for: 4 -> 0; matrix products, arithmetic and copies ran while one was open for 1% -> 0% of each run, Pallas kernels for 0% -> 0%
where the time goes in v1:
time: 111 us
  Pallas kernels  104 us (94%)
  local copies, waits for them, and re-layouts  6.09 us (5%)
    pallas_call x1, Pallas kernels, body(): pl.pallas_call(functools.partial(kernel, ring_z, reps), out_shape=jax.Sha...  104 us
    unnamed x19, local copies, waits for them, and re-layouts  6.09 us

profile of v1, /device:TPU:1, one launch (start us, length us, event | category | flops | bytes accessed | tf_op | source)
XLA Modules:
  0.0 110.5 jit_solution(4357385632622165072)
XLA Ops:
  0.7 0.0 copy-start.7
  0.7 0.0 copy-start.8
  0.7 0.0 copy-start.5
  0.7 0.0 copy-start.6
  0.7 0.6 copy-done.7
  1.3 0.0 copy-done.8
  1.3 0.0 copy-done.5
  1.4 0.0 copy-done.6
  1.4 0.0 copy-start
  1.4 1.2 %copy-done = bf16[1,1,32,128,128]{4,3,2,1,0:T(8,128)(2,1)S(1)} copy-done((bf16[1,1,32,128,128]{4,3,2,1,0:T(8,128)(2,1)S(1)}, bf16[1,1,32,128,128]{4,3,2,1,0:T(8,128)(2,1)}, u32[]{:S(2)}) %copy-start) | copy-done | bytes 1048600
  2.6 0.0 copy-start.1
  2.6 0.9 copy-done.1
  3.5 0.0 copy-start.2
  3.5 0.9 copy-done.2
  4.4 0.0 copy-start.3
  4.4 0.9 copy-done.3
  5.3 0.0 copy-start.4
  5.3 0.8 copy-done.4
  6.1 103.7 %shard_map.100 = bf16[1,128,256]{2,1,0:T(8,128)(2,1)S(1)} custom-call(bf16[128,256]{1,0:T(8,128)(2,1)S(1)} %copy-done.4, s32[1,128]{1,0:T(1,128)S(1)} %bitcast.3, bf16[256,256]{1,0:T(8,128)(2,1)S(1)} %copy-done.1, bf16[1,256,256]{2,1,0:T(8,128)(2,1)S(1)} %copy-done.2, bf16[1,256,256]{2,1,0:T(8,128)(2,1)S(1)} %copy-done.3, f32[1,256]{1,0:T(1,128)S(1)} %bitcast.2, ...), custom_call_target="tpu_custom_call" | custom-call | tf_op jit(solution)/shard_map/pallas_call | solution.py:364
  109.9 0.6 copy.13
Async XLA Ops:
  0.7 0.7 copy-start.7
  0.7 0.7 copy-start.8
  0.7 0.7 copy-start.5
  0.7 0.7 copy-start.6
  1.4 1.2 %copy-start = (bf16[1,1,32,128,128]{4,3,2,1,0:T(8,128)(2,1)S(1)}, bf16[1,1,32,128,128]{4,3,2,1,0:T(8,128)(2,1)}, u32[]{:S(2)}) copy-start(bf16[1,1,32,128,128]{4,3,2,1,0:T(8,128)(2,1)} %tile_values.1) | copy-start | bytes 3145732
  2.6 0.9 copy-start.1
  3.5 0.9 copy-start.2
  4.4 0.9 copy-start.3
  5.3 0.8 copy-start.4

commit v2 on v1

--- a/solution.py
+++ b/solution.py
@@ -9,7 +9,8 @@
 
 MESH = pl.DeviceIdType.MESH
 RING_Y = 4
-ROWS_A = 48
+ROWS_A = 64
+STRIDE = 3
 F32 = jnp.float32
 BF16 = jnp.bfloat16
 
@@ -17,17 +18,24 @@
 def kernel(
     ring_z,
     reps,
+    features_in,
+    class_ids_in,
+    label_table_in,
+    self_weight,
+    neighbor_weight,
+    norm_scale_in,
+    tile_values,
+    block_row_in,
+    section_in,
+    count_in,
+    out,
     features,
     class_ids,
     label_table,
-    self_weight,
-    neighbor_weight,
     norm_scale,
-    tile_values,
     block_row,
     section,
     count,
-    out,
     tiles,
     placed,
     panels,
@@ -44,7 +52,7 @@
     degree_arrived,
     send_sem,
     recv_sem,
-    tile_sem,
+    load_sem,
 ):
     slots = tiles.shape[0]
     edge = tiles.shape[1]
@@ -62,10 +70,7 @@
         return ((core + dc) % 2, to_row, (rep + dr) % reps)
 
     def z_slot(d):
-        d = d % ring_z
-        if d < half_z:
-            return 2 * d
-        return ring_z - 1 if d == half_z else 2 * (ring_z - d) - 1
+        return (d + half_z - 1) % ring_z
 
     started = []
 
@@ -83,16 +88,36 @@
         started.append(copy)
         return copy
 
-    tile_copy = pltpu.make_async_copy(tile_values.at[0, 0], tiles, tile_sem)
-    tile_copy.start()
+    loads = [
+        pltpu.make_async_copy(src, dst, load_sem.at[i])
+        for i, (src, dst) in enumerate(
+            [
+                (class_ids_in, class_ids),
+                (label_table_in, label_table),
+                (features_in, features),
+                (block_row_in, block_row),
+                (section_in, section),
+                (count_in, count),
+                (norm_scale_in, norm_scale),
+                (tile_values.at[0, 0], tiles),
+                (self_weight.at[0], weights.at[core, 0]),
+                (neighbor_weight.at[0], weights.at[core, 1]),
+            ]
+        )
+    ]
+    for load in loads:
+        load.start()
 
     barrier = pltpu.get_barrier_semaphore()
-    friends = [device(dz=1), device(dz=-1), device(dy=1), device(dy=-1), device(dy=2), device(dc=1)]
+    friends = [device(dz=d) for d in (1, -1, 2, -2, STRIDE, -STRIDE)]
+    friends += [device(dy=1), device(dy=-1), device(dy=2), device(dc=1)]
     for j in range(1, reps):
         friends += [device(dr=j), device(dr=j, dc=1)]
     for friend in friends:
         pl.semaphore_signal(barrier, inc=1, device_id=friend, device_id_type=MESH)
 
+    for load in loads[:3]:
+        load.wait()
     classes = label_table.shape[0]
     one_hot = (
         lax.broadcasted_iota(jnp.int32, (classes, edge), 0) == class_ids[...]
@@ -109,83 +134,93 @@
     def gather(layer, whole, work):
         a, b = parts_a[layer], parts_b[layer]
         mine = own_half(whole)
-        a[0] = mine[:rows_a]
-        b[0, 0] = mine[rows_a:]
+        a[z_slot(0) * RING_Y] = mine[:rows_a]
+        b[0, z_slot(0)] = mine[rows_a:]
         if layer == 0:
             pl.semaphore_wait(barrier, len(friends))
 
-        def b_ring(s):
-            cut = 48 if rows_b >= 64 else rows_b // 2
-            if s < half_z:
-                up, down = slice(None), slice(None)
-            else:
-                up, down = slice(0, cut), slice(cut, rows_b)
-            return (
-                send(b.at[0, z_slot(1 - s), up], b.at[0, z_slot(-s), up], device(dz=1)),
-                send(b.at[0, z_slot(s - 1), down], b.at[0, z_slot(s), down], device(dz=-1)),
-            )
-
-        def a_ring(s):
-            def block(d, part):
-                at = z_slot(d) * RING_Y
-                if s < half_z:
-                    return a.at[pl.ds(at, RING_Y)]
-                return a.at[pl.ds(at + part * (RING_Y // 2), RING_Y // 2)]
-
-            return (
-                send(block(1 - s, 0), block(-s, 0), device(dz=1)),
-                send(block(s - 1, 1), block(s, 1), device(dz=-1)),
-            )
-
-        def b_side(s):
-            if s == 0:
-                at = pl.ds(0, 1)
-            elif s < half_z:
-                at = pl.ds(2 * s - 1, 2)
-            else:
-                at = pl.ds(ring_z - 1, 1)
-            copies = [
-                send(b.at[0, at], b.at[RING_Y - 1, at], device(dy=1)),
-                send(b.at[0, at], b.at[1, at], device(dy=-1)),
+        def along_y(src_of, dst_of):
+            return [
+                send(src_of, dst_of((RING_Y - dy) % RING_Y), device(dy=dy)) for dy in (2, 1, -1)
             ]
-            if s == half_z:
-                copies.append(send(b.at[0, at], b.at[2, at], device(dy=2)))
-            return copies
-
-        def b_far(s):
-            copies = [send(b.at[RING_Y - 1, max(2 * s - 1, 0)], b.at[2, max(2 * s - 1, 0)], device(dy=1))]
-            if s > 0:
-                copies.append(send(b.at[1, 2 * s], b.at[2, 2 * s], device(dy=-1)))
-            return copies
-
-        a_side = [
-            send(a.at[0], a.at[(RING_Y - dy) % RING_Y], device(dy=dy)) for dy in (1, -1, 2)
-        ]
-        b_now = b_ring(1)
-        side = b_side(0)
+
+        def block(d):
+            return a.at[pl.ds(z_slot(d) * RING_Y, RING_Y)]
+
+        def chain(d, up):
+            to = d - STRIDE if up else d + STRIDE
+            target = device(dz=STRIDE if up else -STRIDE)
+            return [
+                send(
+                    a.at[z_slot(d) * RING_Y],
+                    a.at[z_slot(to) * RING_Y],
+                    target,
+                ),
+                send(b.at[0, z_slot(d)], b.at[0, z_slot(to)], target),
+            ]
+
+        def a_spread(d):
+            at = z_slot(d) * RING_Y
+            return along_y(a.at[at], lambda e: a.at[at + e])
+
+        def a_local(d):
+            return [
+                send(block(d), block(d - 1), device(dz=1)),
+                send(block(d), block(d + 1), device(dz=-1)),
+            ]
+
+        def b_local(d):
+            at = z_slot(d)
+            return [
+                send(b.at[0, at], b.at[0, at - 1], device(dz=1)),
+                send(b.at[0, at], b.at[0, at + 1], device(dz=-1)),
+            ]
+
+        def b_spread(d, many=3):
+            at = pl.ds(z_slot(d) - many // 2, many)
+            return along_y(b.at[0, at], lambda e: b.at[e, at])
+
+        def wait(copies):
+            for copy in copies:
+                copy.wait_recv()
+
+        steps = (ring_z - 1) // STRIDE // 2
         last = []
-        for copy in a_side:
-            copy.wait_recv()
-        a_now = a_ring(1)
-        work(0)
-        for s in range(1, half_z + 1):
-            for copy in b_now:
-                copy.wait_recv()
-            if s < half_z:
-                b_now = b_ring(s + 1)
-            side_next = b_side(s)
-            for copy in a_now:
-                copy.wait_recv()
-            if s < half_z:
-                a_now = a_ring(s + 1)
-            for copy in side:
-                copy.wait_recv()
-            last += b_far(s - 1)
-            side = side_next
-            work(s)
-        for copy in side + last:
-            copy.wait_recv()
-
+        relays = [0]
+        for step in range(steps + 1):
+            ahead = []
+            if step < steps:
+                ahead = chain(relays[0], True) + chain(relays[-1], False)
+            near, side = [], []
+            for d in relays:
+                near += b_local(d)
+                side += a_spread(d)
+            if step == steps:
+                near.append(
+                    send(
+                        b.at[0, z_slot(relays[0])],
+                        b.at[0, ring_z - 1],
+                        device(dz=2),
+                    )
+                )
+            work(2 * step)
+            wait(near[: 2 * len(relays)])
+            for d in relays:
+                last += b_spread(d)
+            wait(side)
+            for d in relays:
+                last += a_local(d)
+            if step == steps:
+                last.append(send(block(relays[-1]), block(half_z), device(dz=-2)))
+                wait(near[2 * len(relays) :])
+                last += b_spread(half_z, 1)
+            work(2 * step + 1)
+            wait(ahead)
+            relays = [-STRIDE * (step + 1), STRIDE * (step + 1)]
+        wait(last)
+
+    for load in loads[3:]:
+        load.wait()
     filled = count[0, 0]
     targets = [(block_row[0, 0, k] - rep + reps) % reps for k in range(slots)]
     per_step = max(slots // 4, 1)
@@ -208,29 +243,20 @@
         else:
             degree[...] += sums
 
-    steps = slots // per_step
-
-    def first_work(s):
-        if s == 0:
-            weights[core, 0] = self_weight[0]
-            weights[core, 1] = neighbor_weight[0]
+    pieces = slots // per_step
+
+    def first_work(at):
+        if at == 0:
             hidden.append(send(weights.at[core], weights.at[core], device(dc=1)))
-            tile_copy.wait()
-        if half_z >= 8:
-            if 1 <= s <= steps:
-                place(s - 1)
-            final = s == steps + 1
-        else:
-            if s == 0:
-                for step in range(steps):
-                    place(step)
-            final = s == 1
-        if final:
+            for piece in range(pieces // 2):
+                place(piece)
+        if at == 1:
+            for piece in range(pieces // 2, pieces):
+                place(piece)
             for j in range(1, reps):
                 hidden.append(
                     send(degree.at[pl.ds(j * edge, edge)], degree_arrived.at[j - 1], device(dr=j))
                 )
-        if s == half_z:
             hidden[0].wait_recv()
             own_product[...] = jnp.dot(nodes[0], weights[0, 0], preferred_element_type=F32)
 
@@ -241,11 +267,8 @@
     def aggregate(layer):
         a, b = parts_a[layer], parts_b[layer]
         for k in range(slots):
-            d = (section[0, 0, k] // RING_Y - z + ring_z) % ring_z
+            at = (section[0, 0, k] // RING_Y - z + ring_z + half_z - 1) % ring_z
             e = (section[0, 0, k] % RING_Y - y + RING_Y) % RING_Y
-            at = jnp.where(
-                d < half_z, 2 * d, jnp.where(d == half_z, ring_z - 1, 2 * (ring_z - d) - 1)
-            )
             panels[pl.ds(k * edge, rows_a), :] = a[at * RING_Y + e]
             panels[pl.ds(k * edge + rows_a, rows_b), :] = b[e, at]
         copies = []
@@ -359,14 +382,22 @@
         half = width // 2
         rows_b = edge - ROWS_A
         vmem = pl.BlockSpec(memory_space=pltpu.VMEM)
-        smem = pl.BlockSpec(memory_space=pltpu.SMEM)
+        hbm = pl.BlockSpec(memory_space=pltpu.HBM)
+        classes = label_table.shape[0]
         copies = 2 * (3 + 6 * ring_z) + 8 * reps + 16
         return pl.pallas_call(
             functools.partial(kernel, ring_z, reps),
             out_shape=jax.ShapeDtypeStruct((1, edge, width), BF16),
-            in_specs=[vmem] * 6 + [pl.BlockSpec(memory_space=pl.ANY)] + [smem] * 3,
+            in_specs=[hbm] * 10,
             out_specs=vmem,
             scratch_shapes=[
+                pltpu.VMEM((edge, width), BF16),
+                pltpu.VMEM((1, edge), jnp.int32),
+                pltpu.VMEM((classes, width), BF16),
+                pltpu.VMEM((1, width), F32),
+                pltpu.SMEM((1, 1, slots), jnp.int32),
+                pltpu.SMEM((1, 1, slots), jnp.int32),
+                pltpu.SMEM((1, 1), jnp.int32),
                 pltpu.VMEM((slots, edge, edge), BF16),
                 pltpu.VMEM((reps * edge, slots * edge), BF16),
                 pltpu.VMEM((slots * edge, half), BF16),
@@ -383,10 +414,10 @@
                 pltpu.VMEM((reps - 1, edge, half), F32),
                 pltpu.SemaphoreType.DMA((copies,)),
                 pltpu.SemaphoreType.DMA((copies,)),
-                pltpu.SemaphoreType.DMA,
+                pltpu.SemaphoreType.DMA((10,)),
             ],
             compiler_params=pltpu.CompilerParams(
-                collective_id=0, has_side_effects=True, vmem_limit_bytes=40 * 2**20
+                collective_id=0, has_side_effects=True, vmem_limit_bytes=64 * 2**20
             ),
         )(
             features,

time: 111 us -> 82.6 us (0.74)
  Pallas kernels: 104 us -> 80.2 us
  local copies, waits for them, and re-layouts: 6.09 us -> 1.47 us
    pallas_call x1, Pallas kernels: 104 us -> 80.2 us  [body(): pl.pallas_call(functools.partial(kernel, ring_z, reps), out_shape=jax.Sha...]
    unnamed x19 -> x1, local copies, waits for them, and re-layouts: 6.09 us -> 1.47 us
where the time goes in v2:
time: 82.6 us; the launch traced here: 82.4 us
  Pallas kernels  80.2 us (97%)
  local copies, waits for them, and re-layouts  1.47 us (2%)
    pallas_call x1, Pallas kernels, body(): pl.pallas_call(functools.partial(kernel, ring_z, reps), out_shape=jax.Sha...  80.2 us

profile of v2, /device:TPU:1, one launch (start us, length us, event | category | flops | bytes accessed | tf_op | source)
XLA Modules:
  0.0 82.4 jit_solution(10946708733960922343)
XLA Ops:
  0.7 80.2 %shard_map.100 = bf16[1,128,256]{2,1,0:T(8,128)(2,1)} custom-call(bf16[128,256]{1,0:T(8,128)(2,1)} %features_in.1, s32[1,128]{1,0:T(1,128)} %bitcast.3, bf16[256,256]{1,0:T(8,128)(2,1)} %label_table_in.1, bf16[1,256,256]{2,1,0:T(8,128)(2,1)} %self_weight.1, bf16[1,256,256]{2,1,0:T(8,128)(2,1)} %neighbor_weight.1, f32[1,256]{1,0:T(1,128)} %bitcast.2, ...), custom_call_target="tpu_custom_call" | custom-call | tf_op jit(solution)/shard_map/pallas_call | solution.py:388
  80.9 1.5 %copy.13 = bf16[1,128,256]{2,1,0:T(8,128)(2,1)} copy(bf16[1,128,256]{2,1,0:T(8,128)(2,1)} %shard_map.100) | data formatting | bytes 131072

commit v3 on v2

--- a/solution.py
+++ b/solution.py
@@ -10,9 +10,15 @@
 MESH = pl.DeviceIdType.MESH
 RING_Y = 4
 ROWS_A = 64
-STRIDE = 3
+RELAYS = [(-3, 0), (3, 0), (-6, -3), (6, 3)]
+LOCALS = [1, -1]
+FAR_FROM = -6
 F32 = jnp.float32
 BF16 = jnp.bfloat16
+
+
+def far_step(ring_z):
+    return ring_z // 2 + FAR_FROM if ring_z > 4 else 2
 
 
 def kernel(
@@ -39,10 +45,8 @@
     tiles,
     placed,
     panels,
-    first_a,
-    first_b,
-    second_a,
-    second_b,
+    first_chunks,
+    second_chunks,
     weights,
     nodes,
     own_product,
@@ -56,9 +60,8 @@
 ):
     slots = tiles.shape[0]
     edge = tiles.shape[1]
-    parts_a, parts_b = (first_a, second_a), (first_b, second_b)
-    rows_a, half_f = first_a.shape[1:]
-    rows_b = first_b.shape[2]
+    chunks = (first_chunks, second_chunks)
+    half_f = first_chunks.shape[-1]
     half_z = ring_z // 2
     core = lax.axis_index("layer")
     row = lax.axis_index("row")
@@ -109,7 +112,10 @@
         load.start()
 
     barrier = pltpu.get_barrier_semaphore()
-    friends = [device(dz=d) for d in (1, -1, 2, -2, STRIDE, -STRIDE)]
+    relays = RELAYS if ring_z > 4 else []
+    steps_z = set(LOCALS) | {d - parent for d, parent in relays}
+    steps_z |= {-d for d in steps_z} | {far_step(ring_z), -far_step(ring_z)}
+    friends = [device(dz=d) for d in sorted(steps_z)]
     friends += [device(dy=1), device(dy=-1), device(dy=2), device(dc=1)]
     for j in range(1, reps):
         friends += [device(dr=j), device(dr=j, dc=1)]
@@ -132,92 +138,72 @@
         return jnp.where(core == 0, whole[:, :half_f].astype(F32), whole[:, half_f:].astype(F32)).astype(BF16)
 
     def gather(layer, whole, work):
-        a, b = parts_a[layer], parts_b[layer]
-        mine = own_half(whole)
-        a[z_slot(0) * RING_Y] = mine[:rows_a]
-        b[0, z_slot(0)] = mine[rows_a:]
+        held = chunks[layer]
+        top, bottom = slice(0, ROWS_A), slice(ROWS_A, None)
+        held[z_slot(0) * RING_Y] = own_half(whole)
         if layer == 0:
             pl.semaphore_wait(barrier, len(friends))
 
-        def along_y(src_of, dst_of):
+        def at(d, e=0):
+            return z_slot(d) * RING_Y + e % RING_Y
+
+        def relay(d, to):
+            return send(held.at[at(d)], held.at[at(to)], device(dz=d - to))
+
+        def along_y(d, rows=slice(None)):
             return [
-                send(src_of, dst_of((RING_Y - dy) % RING_Y), device(dy=dy)) for dy in (2, 1, -1)
+                send(held.at[at(d), rows], held.at[at(d, -dy), rows], device(dy=dy))
+                for dy in (2, 1, -1)
             ]
 
-        def block(d):
-            return a.at[pl.ds(z_slot(d) * RING_Y, RING_Y)]
-
-        def chain(d, up):
-            to = d - STRIDE if up else d + STRIDE
-            target = device(dz=STRIDE if up else -STRIDE)
-            return [
-                send(
-                    a.at[z_slot(d) * RING_Y],
-                    a.at[z_slot(to) * RING_Y],
-                    target,
-                ),
-                send(b.at[0, z_slot(d)], b.at[0, z_slot(to)], target),
+        def spread(d):
+            onward = [(to, relay(d, to)) for to, parent in relays if parent == d]
+            near = [
+                (dz, send(held.at[at(d)], held.at[at(d - dz)], device(dz=dz))) for dz in LOCALS
             ]
-
-        def a_spread(d):
-            at = z_slot(d) * RING_Y
-            return along_y(a.at[at], lambda e: a.at[at + e])
-
-        def a_local(d):
-            return [
-                send(block(d), block(d - 1), device(dz=1)),
-                send(block(d), block(d + 1), device(dz=-1)),
-            ]
-
-        def b_local(d):
-            at = z_slot(d)
-            return [
-                send(b.at[0, at], b.at[0, at - 1], device(dz=1)),
-                send(b.at[0, at], b.at[0, at + 1], device(dz=-1)),
-            ]
-
-        def b_spread(d, many=3):
-            at = pl.ds(z_slot(d) - many // 2, many)
-            return along_y(b.at[0, at], lambda e: b.at[e, at])
-
-        def wait(copies):
-            for copy in copies:
+            side = along_y(d)
+            across = []
+            if d == (FAR_FROM if relays else 0):
+                across = [
+                    send(held.at[at(d)], held.at[at(half_z)], device(dz=far_step(ring_z)))
+                ]
+            return onward, near, side, across
+
+        last = []
+
+        def corners(d, near, side):
+            for dz, copy in near:
                 copy.wait_recv()
-
-        steps = (ring_z - 1) // STRIDE // 2
-        last = []
-        relays = [0]
-        for step in range(steps + 1):
-            ahead = []
-            if step < steps:
-                ahead = chain(relays[0], True) + chain(relays[-1], False)
-            near, side = [], []
-            for d in relays:
-                near += b_local(d)
-                side += a_spread(d)
-            if step == steps:
-                near.append(
+                last.extend(along_y(d - dz, bottom))
+            for copy in side:
+                copy.wait_recv()
+            for dz in LOCALS:
+                last.append(
                     send(
-                        b.at[0, z_slot(relays[0])],
-                        b.at[0, ring_z - 1],
-                        device(dz=2),
+                        held.at[pl.ds(at(d, 1), RING_Y - 1), top],
+                        held.at[pl.ds(at(d - dz, 1), RING_Y - 1), top],
+                        device(dz=dz),
                     )
                 )
-            work(2 * step)
-            wait(near[: 2 * len(relays)])
-            for d in relays:
-                last += b_spread(d)
-            wait(side)
-            for d in relays:
-                last += a_local(d)
-            if step == steps:
-                last.append(send(block(relays[-1]), block(half_z), device(dz=-2)))
-                wait(near[2 * len(relays) :])
-                last += b_spread(half_z, 1)
-            work(2 * step + 1)
-            wait(ahead)
-            relays = [-STRIDE * (step + 1), STRIDE * (step + 1)]
-        wait(last)
+
+        coming, near, side, opposite = spread(0)
+        work(0)
+        corners(0, near, side)
+        work(1)
+        pending = []
+        while coming:
+            d, copy = coming.pop(0)
+            copy.wait_recv()
+            onward, near, side, across = spread(d)
+            coming += onward
+            opposite += across
+            pending.append((d, near, side))
+        for entry in pending:
+            corners(*entry)
+        opposite[0].wait_recv()
+        last.extend(along_y(half_z))
+        for copy in last:
+            copy.wait_recv()
 
     for load in loads[3:]:
         load.wait()
@@ -265,12 +251,11 @@
             own_product[...] = jnp.dot(nodes[1], weights[1, 0], preferred_element_type=F32)
 
     def aggregate(layer):
-        a, b = parts_a[layer], parts_b[layer]
+        held = chunks[layer]
         for k in range(slots):
             at = (section[0, 0, k] // RING_Y - z + ring_z + half_z - 1) % ring_z
             e = (section[0, 0, k] % RING_Y - y + RING_Y) % RING_Y
-            panels[pl.ds(k * edge, rows_a), :] = a[at * RING_Y + e]
-            panels[pl.ds(k * edge + rows_a, rows_b), :] = b[e, at]
+            panels[pl.ds(k * edge, edge), :] = held[at * RING_Y + e]
         copies = []
         for j in [reps // 2] + [j for j in range(1, reps) if j != reps // 2] + [0]:
             total = jnp.dot(
@@ -380,7 +365,6 @@
         slots, edge = tile_values.shape[2:4]
         width = features.shape[1]
         half = width // 2
-        rows_b = edge - ROWS_A
         vmem = pl.BlockSpec(memory_space=pltpu.VMEM)
         hbm = pl.BlockSpec(memory_space=pltpu.HBM)
         classes = label_table.shape[0]
@@ -401,10 +385,8 @@
                 pltpu.VMEM((slots, edge, edge), BF16),
                 pltpu.VMEM((reps * edge, slots * edge), BF16),
                 pltpu.VMEM((slots * edge, half), BF16),
-                pltpu.VMEM((ring_z * RING_Y, ROWS_A, half), BF16),
-                pltpu.VMEM((RING_Y, ring_z, rows_b, half), BF16),
-                pltpu.VMEM((ring_z * RING_Y, ROWS_A, half), BF16),
-                pltpu.VMEM((RING_Y, ring_z, rows_b, half), BF16),
+                pltpu.VMEM((ring_z * RING_Y, edge, half), BF16),
+                pltpu.VMEM((ring_z * RING_Y, edge, half), BF16),
                 pltpu.VMEM((2, 2, width, width), BF16),
                 pltpu.VMEM((2, edge, width), BF16),
                 pltpu.VMEM((edge, width), F32),

time: 82.6 us -> 76.9 us (0.931)
  Pallas kernels: 80.2 us -> 74.5 us
    pallas_call x1, Pallas kernels: 80.2 us -> 74.5 us  [body(): pl.pallas_call(functools.partial(kernel, ring_z, reps), out_shape=jax.Sha...]
where the time goes in v3:
time: 76.9 us; the launch traced here: 76.7 us
  Pallas kernels  74.5 us (97%)
  local copies, waits for them, and re-layouts  1.47 us (2%)
    pallas_call x1, Pallas kernels, body(): pl.pallas_call(functools.partial(kernel, ring_z, reps), out_shape=jax.Sha...  74.5 us

profile of v3, /device:TPU:1, one launch (start us, length us, event | category | flops | bytes accessed | tf_op | source)
XLA Modules:
  0.0 76.7 jit_solution(621680150129667033)
XLA Ops:
  0.7 74.5 %shard_map.100 = bf16[1,128,256]{2,1,0:T(8,128)(2,1)} custom-call(bf16[128,256]{1,0:T(8,128)(2,1)} %features_in.1, s32[1,128]{1,0:T(1,128)} %bitcast.3, bf16[256,256]{1,0:T(8,128)(2,1)} %label_table_in.1, bf16[1,256,256]{2,1,0:T(8,128)(2,1)} %self_weight.1, bf16[1,256,256]{2,1,0:T(8,128)(2,1)} %neighbor_weight.1, f32[1,256]{1,0:T(1,128)} %bitcast.2, ...), custom_call_target="tpu_custom_call" | custom-call | tf_op jit(solution)/shard_map/pallas_call | solution.py:372
  75.2 1.5 %copy.13 = bf16[1,128,256]{2,1,0:T(8,128)(2,1)} copy(bf16[1,128,256]{2,1,0:T(8,128)(2,1)} %shard_map.100) | data formatting | bytes 131072

commit v4 on v3

--- a/solution.py
+++ b/solution.py
@@ -158,15 +158,15 @@
 
         def spread(d):
             onward = [(to, relay(d, to)) for to, parent in relays if parent == d]
-            near = [
-                (dz, send(held.at[at(d)], held.at[at(d - dz)], device(dz=dz))) for dz in LOCALS
-            ]
-            side = along_y(d)
             across = []
             if d == (FAR_FROM if relays else 0):
                 across = [
                     send(held.at[at(d)], held.at[at(half_z)], device(dz=far_step(ring_z)))
                 ]
+            near = [
+                (dz, send(held.at[at(d)], held.at[at(d - dz)], device(dz=dz))) for dz in LOCALS
+            ]
+            side = along_y(d)
             return onward, near, side, across
 
         last = []
@@ -198,10 +198,12 @@
             coming += onward
             opposite += across
             pending.append((d, near, side))
-        for entry in pending:
+        for entry in pending[:-2]:
             corners(*entry)
         opposite[0].wait_recv()
         last.extend(along_y(half_z))
+        for entry in pending[-2:]:
+            corners(*entry)
         for copy in last:
             copy.wait_recv()
 
@@ -399,7 +401,7 @@
                 pltpu.SemaphoreType.DMA((10,)),
             ],
             compiler_params=pltpu.CompilerParams(
-                collective_id=0, has_side_effects=True, vmem_limit_bytes=64 * 2**20
+                collective_id=0, has_side_effects=True, vmem_limit_bytes=56442880
             ),
         )(
             features,

time: 76.9 us -> 75.8 us (0.986)
  Pallas kernels: 74.5 us -> 73.6 us
    pallas_call x1, Pallas kernels: 74.5 us -> 73.6 us  [body(): pl.pallas_call(functools.partial(kernel, ring_z, reps), out_shape=jax.Sha...]
where the time goes in v4:
time: 75.8 us; the launch traced here: 75.7 us
  Pallas kernels  73.6 us (97%)
  local copies, waits for them, and re-layouts  1.31 us (2%)
    pallas_call x1, Pallas kernels, body(): pl.pallas_call(functools.partial(kernel, ring_z, reps), out_shape=jax.Sha...  73.6 us

profile of v4, /device:TPU:1, one launch (start us, length us, event | category | flops | bytes accessed | tf_op | source)
XLA Modules:
  0.0 75.7 jit_solution(15062073965293580303)
XLA Ops:
  0.7 0.0 copy-start.2
  0.7 0.0 copy-start.3
  0.7 0.0 copy-start
  0.7 0.0 copy-start.1
  0.7 0.6 copy-done.2
  1.3 0.0 copy-done.3
  1.3 0.0 copy-done
  1.4 0.0 copy-done.1
  1.4 73.6 %shard_map.100 = bf16[1,128,256]{2,1,0:T(8,128)(2,1)S(1)} custom-call(bf16[128,256]{1,0:T(8,128)(2,1)} %features_in.1, s32[1,128]{1,0:T(1,128)S(1)} %bitcast.3, bf16[256,256]{1,0:T(8,128)(2,1)} %label_table_in.1, bf16[1,256,256]{2,1,0:T(8,128)(2,1)} %self_weight.1, bf16[1,256,256]{2,1,0:T(8,128)(2,1)} %neighbor_weight.1, f32[1,256]{1,0:T(1,128)S(1)} %bitcast.2, ...), custom_call_target="tpu_custom_call" | custom-call | tf_op jit(solution)/shard_map/pallas_call | solution.py:374
  75.0 0.6 copy.13
Async XLA Ops:
  0.7 0.7 copy-start.2
  0.7 0.7 copy-start.3
  0.7 0.7 copy-start
  0.7 0.7 copy-start.1

commit v5 on v4

--- a/solution.py
+++ b/solution.py
@@ -207,10 +207,7 @@
         for copy in last:
             copy.wait_recv()
 
-    for load in loads[3:]:
-        load.wait()
-    filled = count[0, 0]
-    targets = [(block_row[0, 0, k] - rep + reps) % reps for k in range(slots)]
+    filled, targets = [], []
     per_step = max(slots // 4, 1)
     ones = jnp.ones((per_step * edge, half_f), BF16)
     hidden = []
@@ -219,7 +216,7 @@
         for k in range(step * per_step, (step + 1) * per_step):
             tile = tiles[k]
             for j in range(reps):
-                keep = jnp.logical_and(targets[k] == j, k < filled)
+                keep = jnp.logical_and(targets[k] == j, k < filled[0])
                 placed[pl.ds(j * edge, edge), pl.ds(k * edge, edge)] = jnp.where(
                     keep, tile, jnp.zeros_like(tile)
                 )
@@ -235,6 +232,10 @@
 
     def first_work(at):
         if at == 0:
+            for load in loads[3:]:
+                load.wait()
+            filled.append(count[0, 0])
+            targets.extend((block_row[0, 0, k] - rep + reps) % reps for k in range(slots))
             hidden.append(send(weights.at[core], weights.at[core], device(dc=1)))
             for piece in range(pieces // 2):
                 place(piece)

time: 75.8 us -> 75.8 us (level)
  no operation moved by 1% of the time
where the time goes in v5:
time: 75.8 us; the launch traced here: 75.6 us
  Pallas kernels  73.6 us (97%)
  local copies, waits for them, and re-layouts  1.31 us (2%)
    pallas_call x1, Pallas kernels, body(): pl.pallas_call(functools.partial(kernel, ring_z, reps), out_shape=jax.Sha...  73.6 us

profile of v5, /device:TPU:1, one launch (start us, length us, event | category | flops | bytes accessed | tf_op | source)
XLA Modules:
  0.0 75.6 jit_solution(7709113676673548064)
XLA Ops:
  0.7 0.0 copy-start.2
  0.7 0.0 copy-start.3
  0.7 0.0 copy-start
  0.7 0.0 copy-start.1
  0.7 0.6 copy-done.2
  1.3 0.0 copy-done.3
  1.3 0.0 copy-done
  1.4 0.0 copy-done.1
  1.4 73.6 %shard_map.100 = bf16[1,128,256]{2,1,0:T(8,128)(2,1)S(1)} custom-call(bf16[128,256]{1,0:T(8,128)(2,1)} %features_in.1, s32[1,128]{1,0:T(1,128)S(1)} %bitcast.3, bf16[256,256]{1,0:T(8,128)(2,1)} %label_table_in.1, bf16[1,256,256]{2,1,0:T(8,128)(2,1)} %self_weight.1, bf16[1,256,256]{2,1,0:T(8,128)(2,1)} %neighbor_weight.1, f32[1,256]{1,0:T(1,128)S(1)} %bitcast.2, ...), custom_call_target="tpu_custom_call" | custom-call | tf_op jit(solution)/shard_map/pallas_call | solution.py:375
  75.0 0.6 copy.13
Async XLA Ops:
  0.7 0.7 copy-start.2
  0.7 0.7 copy-start.3
  0.7 0.7 copy-start
  0.7 0.7 copy-start.1

commit v6 on v5

--- a/solution.py
+++ b/solution.py
@@ -9,7 +9,7 @@
 
 MESH = pl.DeviceIdType.MESH
 RING_Y = 4
-ROWS_A = 64
+ROWS_A = 80
 RELAYS = [(-3, 0), (3, 0), (-6, -3), (6, 3)]
 LOCALS = [1, -1]
 FAR_FROM = -6

time: 75.8 us -> 75.1 us (level)
  no operation moved by 1% of the time
where the time goes in v6:
time: 75.1 us; the launch traced here: 75 us
  Pallas kernels  72.9 us (97%)
  local copies, waits for them, and re-layouts  1.31 us (2%)
    pallas_call x1, Pallas kernels, body(): pl.pallas_call(functools.partial(kernel, ring_z, reps), out_shape=jax.Sha...  72.9 us

profile of v6, /device:TPU:1, one launch (start us, length us, event | category | flops | bytes accessed | tf_op | source)
XLA Modules:
  0.0 75.0 jit_solution(2834091426157827063)
XLA Ops:
  0.7 0.0 copy-start.2
  0.7 0.0 copy-start.3
  0.7 0.0 copy-start
  0.7 0.0 copy-start.1
  0.7 0.6 copy-done.2
  1.3 0.0 copy-done.3
  1.3 0.0 copy-done
  1.4 0.0 copy-done.1
  1.4 72.9 %shard_map.100 = bf16[1,128,256]{2,1,0:T(8,128)(2,1)S(1)} custom-call(bf16[128,256]{1,0:T(8,128)(2,1)} %features_in.1, s32[1,128]{1,0:T(1,128)S(1)} %bitcast.3, bf16[256,256]{1,0:T(8,128)(2,1)} %label_table_in.1, bf16[1,256,256]{2,1,0:T(8,128)(2,1)} %self_weight.1, bf16[1,256,256]{2,1,0:T(8,128)(2,1)} %neighbor_weight.1, f32[1,256]{1,0:T(1,128)S(1)} %bitcast.2, ...), custom_call_target="tpu_custom_call" | custom-call | tf_op jit(solution)/shard_map/pallas_call | solution.py:375
  74.3 0.6 copy.13
Async XLA Ops:
  0.7 0.7 copy-start.2
  0.7 0.7 copy-start.3
  0.7 0.7 copy-start
  0.7 0.7 copy-start.1
